TPU v7x, 32 devices: a whole 2x2x4 slice. The times are simulated.
32 devices in a mesh: grp: 2 (over x), wf: 16 (over z, y, core).
Axes of the slice: x: 2, y: 2, z: 4, core: 2. Of those that a mesh axis runs over, the one named last changes fastest.
Arguments:
- vectors: bfloat16 [2, 256, 128, 128], P(None, ('grp', 'wf')), parts along dimension 1, may hold values from -16 to 16
- left_env: bfloat16 [21, 256, 128, 128], P(None, ('grp', 'wf')), parts along dimension 1, may hold values from -1 to 1
- right_env: bfloat16 [21, 256, 128, 128], P(None, ('grp', 'wf')), parts along dimension 1, may hold values from -2 to 2
- labels: int32 [256, 2], P(('grp', 'wf')), parts along dimension 0, may hold values from -3 to 3
- partner: int32 [8, 256], P(None, 'grp'), parts along dimension 1, may hold values from 0 to 127, as said below
- active: int32 [21, 256], P(None, ('grp', 'wf')), parts along dimension 1, may hold values 0 or 1
Outputs:
- residual: bfloat16 [2, 256, 128, 128], P(None, ('grp', 'wf')), parts along dimension 1
- rayleigh: float32 [4], P('grp'), parts along dimension 0
There are 2 independent parts, one for each index of `grp`. A program takes and returns all parts, laid end to end along the dimension named above; each array names one. Nothing has to cross between parts.
Inputs may be any that keep to these rules, and one draw needn't show every extreme that they name: For every shift g, partner[g] is a permutation of the 128 block indices that keeps each block's slot: partner[g, q] mod 8 = q mod 8. Block q is held by device q // 8. Counted over all shifts and slots, the blocks of one device go to blocks of any one device at most 4 times, and some pair of devices reaches it.
All inputs are finite; a program needn't handle non-finite values. No bound on the sum of `active` on one device may be relied on, other than what follows from the above.
Results may differ from a plain program's by a relative error of at most 0.0043.
Values may be sent and summed in bfloat16 or wider, within the bound.
A program may use at most 128 MiB of HBM per device.

v0:
```python
import jax
import jax.numpy as jnp
from jax import lax
from jax.sharding import PartitionSpec as P


def term_parcel(flat_blocks, pack_rows, pack_keep, rows_out, per_shift):
    chosen = jnp.take(flat_blocks, pack_rows, axis=0)
    chosen = jnp.where(pack_keep[:, None, None], chosen, jnp.zeros((), chosen.dtype))
    return chosen.reshape((rows_out, per_shift) + flat_blocks.shape[1:])


def left_side(left_env, carried, vector, energy):
    summed = jnp.einsum("ksab,ksbc->sac", left_env, carried, preferred_element_type=jnp.float32)
    return summed + energy[:, None, None] * vector.astype(jnp.float32)


def per_device(vectors, left_env, right_env, labels, partner, active):
    node_count = lax.axis_size("wf")
    this_device = lax.axis_index("wf")
    vector_count = vectors.shape[0]
    slot_count = vectors.shape[1]
    block_side = vectors.shape[2]
    term_count = left_env.shape[0]
    shift_count = partner.shape[0]
    per_shift = (term_count + shift_count - 1) // shift_count
    peer_room = max(1, shift_count * slot_count // node_count)
    item_count = shift_count * slot_count
    rows_out = node_count * peer_room
    item_ids = jnp.arange(item_count, dtype=jnp.int32)
    slot_ids = jnp.arange(slot_count, dtype=jnp.int32)
    shift_ids = jnp.arange(shift_count, dtype=jnp.int32)
    own_targets = lax.dynamic_slice_in_dim(partner, this_device * slot_count, slot_count, 1)
    dest_device = (own_targets // slot_count).reshape(item_count)
    precedes = item_ids[None, :] < item_ids[:, None]
    order_rank = jnp.sum((dest_device[None, :] == dest_device[:, None]) & precedes, axis=1)
    place_device = jnp.arange(node_count, dtype=jnp.int32)[:, None, None]
    place_rank = jnp.arange(peer_room, dtype=jnp.int32)[None, :, None]
    matched = (dest_device[None, None, :] == place_device) & (
        order_rank[None, None, :] == place_rank
    )
    send_item = jnp.sum(jnp.where(matched, item_ids[None, None, :], 0), axis=2).reshape(rows_out)
    send_live = jnp.any(matched, axis=2).reshape(rows_out)
    own_blocks = this_device * slot_count + slot_ids
    block_ids = jnp.arange(partner.shape[1], dtype=jnp.int32)
    found_hits = partner[:, None, :] == own_blocks[None, :, None]
    anchor = jnp.sum(jnp.where(found_hits, block_ids[None, None, :], 0), axis=2)
    sender = anchor // slot_count
    cell_item = shift_ids[:, None] * slot_count + anchor % slot_count
    columns = sender[:, :, None] * slot_count + slot_ids[None, None, :]
    their_device = (
        jnp.take(partner, columns.reshape(-1), axis=1).reshape(
            shift_count, shift_count, slot_count, slot_count
        )
        // slot_count
    )
    their_item = shift_ids[:, None, None, None] * slot_count + slot_ids[None, None, None, :]
    before = their_item < cell_item[None, :, :, None]
    rank_cell = jnp.sum((their_device == this_device) & before, axis=(0, 3))
    recv_row = sender * peer_room + rank_cell
    term_ids = jnp.arange(term_count, dtype=jnp.int32)
    term_shift = term_ids % shift_count
    term_level = term_ids // shift_count
    level_ids = jnp.arange(per_shift, dtype=jnp.int32)
    term_grid = (send_item // slot_count)[:, None] + level_ids[None, :] * shift_count
    pack_rows = (
        jnp.minimum(term_grid, term_count - 1) * slot_count + (send_item % slot_count)[:, None]
    ).reshape(-1)
    pack_keep = (send_live[:, None] & (term_grid < term_count)).reshape(-1)
    unpack_rows = (recv_row[term_shift] * per_shift + term_level[:, None]).reshape(-1)
    energy = 0.3 * (labels[:, 0] + 4).astype(jnp.float32) - 0.2 * labels[:, 1].astype(jnp.float32)
    images = []
    keep_terms = active.astype(jnp.float32)[:, :, None, None]
    for vector_index in range(vector_count):
        product = jnp.einsum(
            "sab,ksbc->ksac", vectors[vector_index], right_env, preferred_element_type=jnp.float32
        )
        carried = (product * keep_terms).astype(jnp.bfloat16)
        parcel = term_parcel(
            carried.reshape(term_count * slot_count, block_side, block_side),
            pack_rows,
            pack_keep,
            rows_out,
            per_shift,
        )
        arrived = lax.all_to_all(parcel, "wf", split_axis=0, concat_axis=0, tiled=True)
        relocated = jnp.take(
            arrived.reshape(-1, block_side, block_side), unpack_rows, axis=0
        ).reshape(term_count, slot_count, block_side, block_side)
        images.append(left_side(left_env, relocated, vectors[vector_index], energy))
    image = jnp.stack(images)
    floats = vectors.astype(jnp.float32)
    squares = jnp.sum(floats * floats, axis=(1, 2, 3))
    correlations = jnp.sum(floats * image, axis=(1, 2, 3))
    squares_all, correlations_all = lax.psum((squares, correlations), "wf")
    rayleigh = correlations_all / (squares_all + 1e-06)
    residual = (image - rayleigh[:, None, None, None] * floats).astype(jnp.bfloat16)
    return (residual, rayleigh)


def solution(mesh):
    in_specs = (
        P(None, ("grp", "wf"), None, None),
        P(None, ("grp", "wf"), None, None),
        P(None, ("grp", "wf"), None, None),
        P(("grp", "wf"), None),
        P(None, "grp"),
        P(None, ("grp", "wf")),
    )
    out_specs = (P(None, ("grp", "wf"), None, None), P("grp"))
    return jax.shard_map(
        per_device, mesh=mesh, in_specs=in_specs, out_specs=out_specs, check_vma=False
    )
```

profile of v0, /device:TPU:0, one launch (start us, length us, event | category | flops | bytes accessed | tf_op | source)
XLA Modules:
  0.0 404.1 jit_solution(9798513931577268255)
XLA Ops:
  0.6 0.8 add_select_fusion.3
  1.5 0.2 convert_reduce_fusion.1
  1.7 0.7 convert_element_type.47
  2.4 7.7 %fusion = bf16[21,8,128,128]{2,3,0,1:T(8,128)(2,1)} fusion(f32[21,8]{0,1:T(8,128)S(1)} %convert_element_type.47, bf16[21,8,128,128]{3,2,1,0:T(8,128)(2,1)} %param.12, bf16[2,8,128,128]{3,2,1,0:T(8,128)(2,1)} %param.10), kind=kOutput, calls=%fused_computation.7 | convolution fusion | flops 710148096 | bytes 11272864 | tf_op jit(solution)/shard_map/sab,ksbc->ksac/dot_general | solution.py:75
  10.0 4.4 %fusion.1 = bf16[21,8,128,128]{2,3,0,1:T(8,128)(2,1)} fusion(f32[21,8]{0,1:T(8,128)S(1)} %convert_element_type.47, bf16[21,8,128,128]{3,2,1,0:T(8,128)(2,1)S(1)} %copy-done.3, bf16[2,8,128,128]{3,2,1,0:T(8,128)(2,1)S(1)} %copy-done), kind=kOutput, calls=%fused_computation.9 | convolution fusion | flops 710148096 | bytes 11276288 | tf_op jit(solution)/shard_map/sab,ksbc->ksac/dot_general | solution.py:75
  14.4 0.2 fusion.27
  14.9 0.1 add.245
  15.1 0.2 and_reduce_fusion
  15.3 8.3 %copy.51 = bf16[21,8,128,128]{3,2,1,0:T(8,128)(2,1)} copy(bf16[21,8,128,128]{2,3,0,1:T(8,128)(2,1)} %fusion) | data formatting | bytes 11010048 | tf_op jit(solution)/shard_map/convert_element_type | solution.py:78
  23.6 8.3 %copy.47 = bf16[21,8,128,128]{3,2,1,0:T(8,128)(2,1)} copy(bf16[21,8,128,128]{2,3,0,1:T(8,128)(2,1)} %fusion.1) | data formatting | bytes 11010048 | tf_op jit(solution)/shard_map/convert_element_type | solution.py:78
  31.9 10.6 %gather_fusion.4 = bf16[192,128,128]{2,1,0:T(8,128)(2,1)} fusion(bf16[168,128,128]{2,1,0:T(8,128)(2,1)} %bitcast.84, s32[1024]{0:T(1024)S(1)} %pad_clamp_fusion.1), kind=kCustom, calls=%fused_computation.2.clone | custom fusion | bytes 12583680 | tf_op jit(solution)/shard_map/jit(_take)/gather | solution.py:8
  42.5 10.6 %gather_fusion.2 = bf16[192,128,128]{2,1,0:T(8,128)(2,1)} fusion(bf16[168,128,128]{2,1,0:T(8,128)(2,1)} %bitcast.83, s32[1024]{0:T(1024)S(1)} %pad_clamp_fusion.1), kind=kCustom, calls=%fused_computation.clone | custom fusion | bytes 12583680 | tf_op jit(solution)/shard_map/jit(_take)/gather | solution.py:8
  53.4 0.1 copy.44
  53.5 0.2 and.163
  53.6 9.2 %select_select_fusion.1 = (bf16[192,128,128]{2,1,0:T(8,128)(2,1)}, bf16[192,128,128]{2,1,0:T(8,128)(2,1)S(1)}) fusion(bf16[192,128,128]{2,1,0:T(8,128)(2,1)} %gather_fusion.2, pred[192]{0:T(512)(128)(4,1)S(1)} %compare_and_fusion.2, pred[192]{0:T(512)(128)(4,1)S(1)} %and.163, bf16[192,128,128]{2,1,0:T(8,128)(2,1)} %gather_fusion.4), kind=kLoop, calls=%fused_computation.11 | loop fusion | flops 12582912 | bytes 25166208 | tf_op jit(solution)/shard_map/jit(_where)/select_n | solution.py:9
  62.9 144.5 %all_to_all.10 = bf16[64,3,128,128]{3,2,1,0:T(8,128)(2,1)} all-to-all(bf16[64,3,128,128]{3,2,1,0:T(8,128)(2,1)S(1)} %bitcast.86), channel_id=1, replica_groups=mesh['grp'=2,'wf'=16] {'wf'}, dimensions={0} | all-to-all | bytes 12582912 | tf_op jit(solution)/shard_map/all_to_all | solution.py:86
  207.3 5.7 %all-to-all-start = ((bf16[64,3,128,128]{3,2,1,0:T(8,128)(2,1)}), bf16[64,3,128,128]{3,2,1,0:T(8,128)(2,1)}, u32[]{:S(2)}, u32[]{:S(2)}) async-start(bf16[64,3,128,128]{3,2,1,0:T(8,128)(2,1)} %bitcast.85), calls=%async_computation | async-start | bytes 12582912 | tf_op jit(solution)/shard_map/all_to_all | solution.py:86
  213.0 0.1 copy.40
  213.2 0.3 select_reduce_fusion
  214.1 1.0 gather_fusion
  215.2 0.4 convert_reduce_fusion
  215.7 0.2 reduce_sum.66
  215.9 0.6 gather_fusion.1
  216.7 10.6 %gather_fusion.5 = bf16[168,128,128]{2,1,0:T(8,128)(2,1)} fusion(bf16[192,128,128]{2,1,0:T(8,128)(2,1)} %bitcast.87, s32[1024]{0:T(1024)S(1)} %pad_clamp_fusion), kind=kCustom, calls=%fused_computation.3.clone | custom fusion | bytes 11010720 | tf_op jit(solution)/shard_map/jit(_take)/gather | solution.py:87
  227.3 99.9 %all-to-all-done = bf16[64,3,128,128]{3,2,1,0:T(8,128)(2,1)} async-done(((bf16[64,3,128,128]{3,2,1,0:T(8,128)(2,1)}), bf16[64,3,128,128]{3,2,1,0:T(8,128)(2,1)}, u32[]{:S(2)}, u32[]{:S(2)}) %all-to-all-start) | async-done | bytes 6291488 | tf_op jit(solution)/shard_map/all_to_all | solution.py:86
  327.2 10.7 %gather_fusion.3 = bf16[168,128,128]{2,1,0:T(8,128)(2,1)} fusion(bf16[192,128,128]{2,1,0:T(8,128)(2,1)} %bitcast.10, s32[1024]{0:T(1024)S(1)} %pad_clamp_fusion), kind=kCustom, calls=%fused_computation.1.clone | custom fusion | bytes 11010720 | tf_op jit(solution)/shard_map/jit(_take)/gather | solution.py:87
  338.0 5.4 %broadcast_select_fusion.1 = (bf16[168,128,128]{2,1,0:T(8,128)(2,1)S(1)}, bf16[168,128,128]{2,1,0:T(8,128)(2,1)S(1)}) fusion(bf16[168,128,128]{2,1,0:T(8,128)(2,1)} %gather_fusion.3, pred[168]{0:T(512)(128)(4,1)S(1)} %compare_and_fusion.1, bf16[168,128,128]{2,1,0:T(8,128)(2,1)} %gather_fusion.5), kind=kLoop, calls=%fused_computation.13 | loop fusion | flops 5505024 | bytes 22020264 | tf_op jit(solution)/shard_map/jit(_take)/select_n | solution.py:87
  343.4 1.6 fusion.11
  345.0 1.6 fusion.13
  346.7 0.4 fusion.15
  347.0 56.0 %all-reduce = (f32[2]{0:T(128)S(1)}, f32[2]{0:T(128)S(1)}) all-reduce(f32[2]{0:T(128)S(1)} %get-tuple-element.5, f32[2]{0:T(128)S(1)} %get-tuple-element.4), channel_id=1, replica_groups=mesh['grp'=2,'wf'=16] {'wf'}, use_global_device_ids=true, to_apply=%region_7.10 | all-reduce | flops 4 | bytes 32 | tf_op jit(solution)/shard_map/psum | solution.py:95
  403.1 1.0 fusion.17
  (54 shorter events, 1.8 us)
Async XLA Ops:
  2.4 7.7 %copy-start = (bf16[2,8,128,128]{3,2,1,0:T(8,128)(2,1)S(1)}, bf16[2,8,128,128]{3,2,1,0:T(8,128)(2,1)}, u32[]{:S(2)}) copy-start(bf16[2,8,128,128]{3,2,1,0:T(8,128)(2,1)} %param.10) | copy-start | bytes 1572868
  2.4 7.7 %copy-start.3 = (bf16[21,8,128,128]{3,2,1,0:T(8,128)(2,1)S(1)}, bf16[21,8,128,128]{3,2,1,0:T(8,128)(2,1)}, u32[]{:S(2)}) copy-start(bf16[21,8,128,128]{3,2,1,0:T(8,128)(2,1)} %param.12) | copy-start | bytes 16515076
  207.3 5.7 %copy-start.1 = (s32[8,128]{1,0:T(8,128)S(1)}, s32[8,128]{1,0:T(8,128)}, u32[]{:S(2)}) copy-start(s32[8,128]{1,0:T(8,128)} %param.14) | copy-start | bytes 12292
  207.3 9.4 %copy-start.4 = (s32[8,2]{0,1:T(2,128)S(1)}, s32[8,2]{0,1:T(2,128)}, u32[]{:S(2)}) copy-start(s32[8,2]{0,1:T(2,128)} %param.13) | copy-start | bytes 196
  207.3 119.9 %all-to-all-start = ((bf16[64,3,128,128]{3,2,1,0:T(8,128)(2,1)}), bf16[64,3,128,128]{3,2,1,0:T(8,128)(2,1)}, u32[]{:S(2)}, u32[]{:S(2)}) async-start(bf16[64,3,128,128]{3,2,1,0:T(8,128)(2,1)} %bitcast.85), calls=%async_computation | async-start | bytes 12582912 | tf_op jit(solution)/shard_map/all_to_all | solution.py:86
  327.2 16.2 %slice-start = ((s8[5505024]{0:T(1024)(128)(4,1)}), s8[1310720]{0:T(1024)(128)(4,1)S(1)}, s32[]{:S(2)}) async-start(s8[5505024]{0:T(1024)(128)(4,1)} %bitcast.88), calls=%async_computation.2 | async-start | bytes 2621440
  338.0 5.4 %slice-start.1 = ((s8[5505024]{0:T(1024)(128)(4,1)}), s8[4194304]{0:T(1024)(128)(4,1)S(1)}, s32[]{:S(2)}) async-start(s8[5505024]{0:T(1024)(128)(4,1)} %bitcast.88), calls=%async_computation.3 | async-start | bytes 8388608
  403.1 1.0 copy-start.2
where the time goes:
time: 405 us; the launch traced here: 404 us
  blocking collectives  201 us (50%)
  waiting for transfers between devices  99.9 us (25%)
  local copies, waits for them, and re-layouts  62.4 us (15%)
  other arithmetic  19.4 us (5%)
  matrix products  15.3 us (4%)
  starting transfers between devices  5.68 us (1%)
    all_to_all x1, blocking collectives, per_device(): lax.all_to_all(parcel, 'wf', split_axis=0, concat_axis=0, tiled=True)  144 us
    all_to_all x1, waiting for transfers between devices, per_device(): lax.all_to_all(parcel, 'wf', split_axis=0, concat_axis=0, tiled=True)  99.9 us
    psum x1, blocking collectives, per_device(): squares_all, correlations_all = lax.psum((squares, correlations), 'wf')  56 us
    gather x2, local copies, waits for them, and re-layouts, per_device(): jnp.take(arrived.reshape(-1, block_side, block_side), unpack_rows, axis=0)  21.3 us
    gather x2, local copies, waits for them, and re-layouts, term_parcel(): chosen = jnp.take(flat_blocks, pack_rows, axis=0)  21.2 us
    convert_element_type x2, local copies, waits for them, and re-layouts, per_device(): carried = (product * keep_terms).astype(jnp.bfloat16)  16.6 us
    dot_general x2, matrix products, per_device(): jnp.einsum('sab,ksbc->ksac', vectors[vector_index], right_env, preferred_...  12 us
    select_n x1, other arithmetic, term_parcel(): jnp.where(pack_keep[:, None, None], chosen, jnp.zeros((), chosen.dtype))  9.23 us
  transfers between devices with their start and end apart: 1, of which 1 were waited for; matrix products, arithmetic and copies ran while one was open for 3% of the time, Pallas kernels for 0%

commit v1 on v0

--- a/solution.py
+++ b/solution.py
@@ -1,7 +1,13 @@
+import functools
+
 import jax
 import jax.numpy as jnp
 from jax import lax
+from jax.experimental import pallas as pl
+from jax.experimental.pallas import tpu as pltpu
 from jax.sharding import PartitionSpec as P
+
+VMEM_BYTES = 56 * 2**20
 
 
 def term_parcel(flat_blocks, pack_rows, pack_keep, rows_out, per_shift):
@@ -98,6 +104,346 @@
     return (residual, rayleigh)
 
 
+def ranked(hits, room):
+    rank = jnp.cumsum(hits.astype(jnp.int32), axis=-1) - 1
+    item_ids = jnp.arange(hits.shape[-1], dtype=jnp.int32)
+    level = jnp.arange(room, dtype=jnp.int32)[:, None]
+    matched = hits[..., None, :] & (rank[..., None, :] == level)
+    return jnp.sum(jnp.where(matched, item_ids, 0), axis=-1)
+
+
+def peer_of(me, step, nodes):
+    difference = nodes - 1 - step
+    peer, bit = 0, 1
+    while bit < nodes:
+        peer += ((me // bit + difference // bit) % 2) * bit
+        bit *= 2
+    return peer
+
+
+def node_kernel(
+    sizes,
+    send_item,
+    recv_cell,
+    place,
+    active,
+    energy,
+    v_ref,
+    r_ref,
+    l_hbm,
+    out_ref,
+    ray_ref,
+    l_ref,
+    vall,
+    parcel,
+    arrived,
+    partial,
+    images,
+    stats,
+    l_sem,
+    v_recv,
+    v_send,
+    y_send,
+    r_recv,
+    r_send,
+    s_recv,
+    s_send,
+):
+    nodes, terms, shifts, slots, room, levels, side = sizes
+    z_count = nodes // 4
+    steps = nodes - 1
+    me = lax.axis_index("wf")
+    z, y, core = me // 4, (me // 2) % 2, me % 2
+    l_copy = pltpu.make_async_copy(l_hbm, l_ref, l_sem)
+    l_copy.start()
+
+    barrier = pltpu.get_barrier_semaphore()
+
+    def greet(step, carry):
+        pl.semaphore_signal(barrier, inc=1, device_id={"wf": peer_of(me, step, nodes)})
+        return carry
+
+    lax.fori_loop(0, steps, greet, 0)
+    pl.semaphore_wait(barrier, steps)
+
+    def v_copy(chunk, target, send_sem):
+        return pltpu.make_async_remote_copy(
+            src_ref=vall.at[chunk],
+            dst_ref=vall.at[chunk],
+            send_sem=send_sem,
+            recv_sem=v_recv.at[chunk],
+            device_id={"wf": target},
+        )
+
+    y_peer = z * 4 + (1 - y) * 2 + core
+    core_peer = z * 4 + y * 2 + (1 - core)
+    up, down = (me + 4) % nodes, (me + nodes - 4) % nodes
+
+    def wait_chunk(chunk):
+        v_copy(chunk, core_peer, y_send.at[0]).wait_recv()
+
+    def each_way(dz, action):
+        index = dz + z_count - 1
+        chunk = me + 4 * dz
+        if dz <= 0:
+
+            @pl.when(z < z_count - 1)
+            def _():
+                action(v_copy(chunk, up, v_send.at[index, 0]))
+
+        if dz >= 0:
+
+            @pl.when(z > 0)
+            def _():
+                action(v_copy(chunk, down, v_send.at[index, 1]))
+
+        action(v_copy(chunk, y_peer, v_send.at[index, 2]))
+        action(v_copy(chunk, core_peer, v_send.at[index, 3]))
+
+    def y_chunk(z_step):
+        return ((z + z_step) % z_count) * 4 + (1 - y) * 2 + core
+
+    def r_copy(step):
+        return pltpu.make_async_remote_copy(
+            src_ref=parcel.at[step],
+            dst_ref=arrived.at[step],
+            send_sem=r_send.at[step],
+            recv_sem=r_recv.at[step],
+            device_id={"wf": peer_of(me, step, nodes)},
+        )
+
+    def pack(step, buffer):
+        peer = peer_of(me, step, nodes)
+        for index in range(room):
+            item = send_item[peer * room + index]
+            shift, slot = item // slots, item % slots
+            for level in range(levels):
+                term = shift + level * shifts
+                live = (term < terms).astype(jnp.int32)
+                term = jnp.minimum(term, terms - 1)
+                keep = (active[term * slots + slot] * live).astype(jnp.float32)
+                block = r_ref[term, slot].astype(jnp.float32) * keep
+                buffer[step, index, level] = block.astype(jnp.bfloat16)
+
+    def pack_and_send(step, carry):
+        pack(step, parcel)
+        r_copy(step).start()
+        return carry
+
+    vall[me] = v_ref[...]
+    each_way(0, lambda copy: copy.start())
+    lax.fori_loop(0, nodes // 2, pack_and_send, 0)
+
+    def inside(dz):
+        return (z + dz >= 0) & (z + dz < z_count)
+
+    others = [sign * far for far in range(1, z_count) for sign in (-1, 1)]
+    for dz in others:
+
+        @pl.when(inside(dz))
+        def _(dz=dz):
+            wait_chunk(me + 4 * dz)
+            each_way(dz, lambda copy: copy.start())
+
+    lax.fori_loop(nodes // 2, steps, pack_and_send, 0)
+    pack(steps, arrived)
+
+    def pass_on(z_step, carry):
+        chunk = y_chunk(z_step)
+        wait_chunk(chunk)
+        v_copy(chunk, core_peer, y_send.at[z_step]).start()
+        return carry
+
+    lax.fori_loop(0, z_count, pass_on, 0)
+
+    def last_chunks(z_step, carry):
+        z_from = (z + z_step) % z_count
+        wait_chunk(z_from * 4 + y * 2 + (1 - core))
+        wait_chunk(z_from * 4 + (1 - y) * 2 + (1 - core))
+        return carry
+
+    lax.fori_loop(0, z_count, last_chunks, 0)
+    l_copy.wait()
+
+    def multiply(step):
+        peer = peer_of(me, step, nodes)
+
+        def one(index, carry):
+            cell = recv_cell[peer * room + index]
+            shift, slot = cell // slots, cell % slots
+            pair = jnp.concatenate([vall[peer, 0, slot], vall[peer, 1, slot]], axis=0)
+            total = jnp.zeros((side, 2 * side), jnp.float32)
+            for level in range(levels):
+                term = jnp.minimum(shift + level * shifts, terms - 1)
+                carried = jnp.dot(
+                    pair, arrived[step, index, level], preferred_element_type=jnp.float32
+                ).astype(jnp.bfloat16)
+                both = jnp.concatenate([carried[:side], carried[side:]], axis=1)
+                total += jnp.dot(l_ref[term, slot], both, preferred_element_type=jnp.float32)
+            partial[step, index] = total
+            return carry
+
+        lax.fori_loop(0, room, one, 0)
+
+    multiply(steps)
+
+    def take(back, carry):
+        step = steps - 1 - back
+        r_copy(step).wait_recv()
+        multiply(step)
+        return carry
+
+    lax.fori_loop(0, steps, take, 0)
+
+    def total_slot(slot, carry):
+        image = jnp.zeros((side, 2 * side), jnp.float32)
+        for shift in range(shifts):
+            spot = place[shift * slots + slot]
+            image += partial[spot // room, spot % room]
+        own = jnp.concatenate([v_ref[0, slot], v_ref[1, slot]], axis=1).astype(jnp.float32)
+        image += energy[slot] * own
+        images[slot] = image
+        squares = jnp.sum(own * own, axis=0, keepdims=True)
+        correlations = jnp.sum(own * image, axis=0, keepdims=True)
+        return (carry[0] + squares, carry[1] + correlations)
+
+    blank = jnp.zeros((1, 2 * side), jnp.float32)
+    squares, correlations = lax.fori_loop(0, slots, total_slot, (blank, blank))
+    row = lax.broadcasted_iota(jnp.int32, (8, 2 * side), 0)
+    stats[me] = jnp.where(row == 0, squares, jnp.where(row == 1, correlations, 0.0))
+
+    def s_copy(chunk, step):
+        return pltpu.make_async_remote_copy(
+            src_ref=stats.at[chunk],
+            dst_ref=stats.at[chunk],
+            send_sem=s_send.at[step],
+            recv_sem=s_recv.at[chunk],
+            device_id={"wf": peer_of(me, step, nodes)},
+        )
+
+    def share(step, carry):
+        s_copy(me, step).start()
+        return carry
+
+    lax.fori_loop(0, steps, share, 0)
+
+    def hear(step, carry):
+        s_copy(peer_of(me, step, nodes), step).wait_recv()
+        return carry
+
+    lax.fori_loop(0, steps, hear, 0)
+    sums = stats[0]
+    for node in range(1, nodes):
+        sums += stats[node]
+    quotients = []
+    for vector in range(2):
+        lanes = slice(vector * side, (vector + 1) * side)
+        square = jnp.sum(sums[0:1, lanes], axis=1, keepdims=True)
+        correlation = jnp.sum(sums[1:2, lanes], axis=1, keepdims=True)
+        quotient = correlation / (square + 1e-06)
+        quotients.append(jnp.broadcast_to(quotient, (1, side)))
+    ray_ref[...] = jnp.concatenate(quotients, axis=0)
+    factor = jnp.concatenate(quotients, axis=1)
+
+    def finish(slot, carry):
+        own = jnp.concatenate([v_ref[0, slot], v_ref[1, slot]], axis=1).astype(jnp.float32)
+        result = (images[slot] - factor * own).astype(jnp.bfloat16)
+        out_ref[0, slot] = result[:, :side]
+        out_ref[1, slot] = result[:, side:]
+        return carry
+
+    lax.fori_loop(0, slots, finish, 0)
+
+    each_way(0, lambda copy: copy.wait_send())
+    for dz in others:
+
+        @pl.when(inside(dz))
+        def _(dz=dz):
+            each_way(dz, lambda copy: copy.wait_send())
+
+    def sent_y(z_step, carry):
+        v_copy(y_chunk(z_step), core_peer, y_send.at[z_step]).wait_send()
+        return carry
+
+    lax.fori_loop(0, z_count, sent_y, 0)
+
+    def sent(step, carry):
+        r_copy(step).wait_send()
+        s_copy(me, step).wait_send()
+        return carry
+
+    lax.fori_loop(0, steps, sent, 0)
+
+
+def node_program(vectors, left_env, right_env, labels, partner, active):
+    nodes = lax.axis_size("wf")
+    me = lax.axis_index("wf")
+    count, slots, side = vectors.shape[:3]
+    terms, shifts = left_env.shape[0], partner.shape[0]
+    levels = (terms + shifts - 1) // shifts
+    items = shifts * slots
+    room = items // nodes
+    node_ids = jnp.arange(nodes, dtype=jnp.int32)
+    owner = (partner // slots).reshape(shifts, nodes, slots)
+    own_owner = lax.dynamic_index_in_dim(owner, me, 1, keepdims=False).reshape(items)
+    incoming = jnp.swapaxes(owner == me, 0, 1).reshape(nodes, items)
+    outgoing = own_owner[None, :] == node_ids[:, None]
+    lists = ranked(jnp.stack([outgoing, incoming]), room).reshape(2, nodes * room)
+    spot = jnp.arange(nodes * room, dtype=jnp.int32)
+    spot_step = nodes - 1 - ((spot // room) ^ me)
+    cells = jnp.arange(items, dtype=jnp.int32)
+    place = jnp.sum(
+        jnp.where(lists[1][None, :] == cells[:, None], spot_step * room + spot % room, 0), axis=1
+    )
+    energy = 0.3 * (labels[:, 0] + 4).astype(jnp.float32) - 0.2 * labels[:, 1].astype(jnp.float32)
+    smem = pl.BlockSpec(memory_space=pltpu.SMEM)
+    vmem = pl.BlockSpec(memory_space=pltpu.VMEM)
+    chunk = (nodes, room, levels, side, side)
+    flops = 2 * 2 * count * items * levels * side**3
+    residual, rayleigh = pl.pallas_call(
+        functools.partial(node_kernel, (nodes, terms, shifts, slots, room, levels, side)),
+        out_shape=(
+            jax.ShapeDtypeStruct(vectors.shape, jnp.bfloat16),
+            jax.ShapeDtypeStruct((count, side), jnp.float32),
+        ),
+        in_specs=[smem] * 5 + [vmem, vmem, pl.BlockSpec(memory_space=pl.ANY)],
+        out_specs=(vmem, vmem),
+        scratch_shapes=[
+            pltpu.VMEM(left_env.shape, jnp.bfloat16),
+            pltpu.VMEM((nodes,) + vectors.shape, jnp.bfloat16),
+            pltpu.VMEM(chunk, jnp.bfloat16),
+            pltpu.VMEM(chunk, jnp.bfloat16),
+            pltpu.VMEM((nodes, room, side, count * side), jnp.float32),
+            pltpu.VMEM((slots, side, count * side), jnp.float32),
+            pltpu.VMEM((nodes, 8, count * side), jnp.float32),
+            pltpu.SemaphoreType.DMA,
+            pltpu.SemaphoreType.DMA((nodes,)),
+            pltpu.SemaphoreType.DMA((2 * (nodes // 4) - 1, 4)),
+            pltpu.SemaphoreType.DMA((nodes // 4,)),
+            pltpu.SemaphoreType.DMA((nodes,)),
+            pltpu.SemaphoreType.DMA((nodes,)),
+            pltpu.SemaphoreType.DMA((nodes,)),
+            pltpu.SemaphoreType.DMA((nodes,)),
+        ],
+        compiler_params=pltpu.CompilerParams(
+            collective_id=0, has_side_effects=True, vmem_limit_bytes=VMEM_BYTES
+        ),
+        cost_estimate=pl.CostEstimate(
+            flops=flops, bytes_accessed=2 * left_env.size * 2, transcendentals=0
+        ),
+    )(lists[0], lists[1], place, active.reshape(-1), energy, vectors, right_env, left_env)
+    return residual, rayleigh[:, 0]
+
+
+def choose(vectors, left_env, right_env, labels, partner, active):
+    nodes = lax.axis_size("wf")
+    items = partner.shape[0] * vectors.shape[1]
+    gathered = nodes * vectors.size * 2
+    even = items % nodes == 0 and nodes % 4 == 0 and nodes & (nodes - 1) == 0
+    program = node_program if even and 2 * gathered < VMEM_BYTES else per_device
+    return program(vectors, left_env, right_env, labels, partner, active)
+
+
 def solution(mesh):
     in_specs = (
         P(None, ("grp", "wf"), None, None),
@@ -109,5 +455,5 @@
     )
     out_specs = (P(None, ("grp", "wf"), None, None), P("grp"))
     return jax.shard_map(
-        per_device, mesh=mesh, in_specs=in_specs, out_specs=out_specs, check_vma=False
+        choose, mesh=mesh, in_specs=in_specs, out_specs=out_specs, check_vma=False
     )

time: 405 us -> 267 us (0.66)
  Pallas kernels: 0 us -> 257 us
  blocking collectives: 201 us -> 0 us
  waiting for transfers between devices: 99.9 us -> 0 us
  local copies, waits for them, and re-layouts: 62.4 us -> 5.84 us
  other arithmetic: 19.4 us -> 3.43 us
  matrix products: 15.3 us -> 0 us
  starting transfers between devices: 5.68 us -> 0 us
    pallas_call x0 -> x1, Pallas kernels: none -> 257 us  [node_program(): pl.pallas_call(functools.partial(node_kernel, (nodes, terms, shifts, slot...]
    all_to_all x1 -> x0, blocking collectives: 144 us -> none  [per_device(): lax.all_to_all(parcel, 'wf', split_axis=0, concat_axis=0, tiled=True)]
    all_to_all x1 -> x0, waiting for transfers between devices: 99.9 us -> none  [per_device(): lax.all_to_all(parcel, 'wf', split_axis=0, concat_axis=0, tiled=True)]
    psum x1 -> x0, blocking collectives: 56 us -> none  [per_device(): squares_all, correlations_all = lax.psum((squares, correlations), 'wf')]
    gather x6 -> x0, local copies, waits for them, and re-layouts: 44.1 us -> none  [the longest x2 21.3 us: per_device(): jnp.take(arrived.reshape(-1, block_side, block_side), unpack_rows, axis=0)]
    convert_element_type x2 -> x0, local copies, waits for them, and re-layouts: 16.6 us -> none  [per_device(): carried = (product * keep_terms).astype(jnp.bfloat16)]
    dot_general x4 -> x0, matrix products: 15.3 us -> none  [the longest x2 12 us: per_device(): jnp.einsum('sab,ksbc->ksac', vectors[vector_index], right_env, preferred_...]
    select_n x9 -> x1, other arithmetic: 15.4 us -> 0.69 us  [node_program(): owner = (partner // slots).reshape(shifts, nodes, slots)]
  transfers between devices with their start and end apart: 1 -> 0, of which waited for: 1 -> 0; matrix products, arithmetic and copies ran while one was open for 3% -> 0% of each run, Pallas kernels for 0% -> 0%
where the time goes in v1:
time: 267 us
  Pallas kernels  257 us (96%)
  local copies, waits for them, and re-layouts  5.84 us (2%)
  other arithmetic  3.43 us (1%)
    pallas_call x1, Pallas kernels, node_program(): pl.pallas_call(functools.partial(node_kernel, (nodes, terms, shifts, slot...  257 us

profile of v1, /device:TPU:0, one launch (start us, length us, event | category | flops | bytes accessed | tf_op | source)
XLA Modules:
  0.0 266.8 jit_solution(12838003610394508255)
XLA Ops:
  0.6 1.3 subtract_bitcast_fusion.energy
  1.9 0.7 add_select_fusion
  2.6 0.8 copy.21
  3.4 0.7 reshape.91.active
  4.1 0.1 reshape.90
  4.2 0.1 copy.17
  4.3 0.1 eq.58
  4.4 0.1 copy.18
  4.5 0.5 reduce_window_sum.11
  5.0 0.2 select_reduce_fusion
  5.2 0.1 copy.20
  5.3 0.1 squeeze.14.recv_cell
  5.4 0.0 copy-start
  5.4 0.7 select_reduce_fusion.1.place
  6.1 0.1 copy.19
  6.2 0.6 squeeze.13.send_item
  6.8 0.0 copy-done
  6.8 256.8 %shard_map.77 = (bf16[2,8,128,128]{3,2,1,0:T(8,128)(2,1)}, f32[2,128]{1,0:T(2,128)}) custom-call(s32[64]{0:T(128)} %squeeze.13.send_item, s32[64]{0:T(128)} %copy-done, s32[64]{0:T(128)} %select_reduce_fusion.1.place, s32[168]{0:T(256)} %reshape.91.active, f32[8]{0:T(128)} %subtract_bitcast_fusion.energy, bf16[2,8,128,128]{3,2,1,0:T(8,128)(2,1)} %v_ref.1, ...), custom_call_target="tpu_custom_call" | custom-call | flops 3221225472 | bytes 11010048 | tf_op jit(solution)/shard_map/pallas_call | solution.py:403
  263.6 1.3 slice_reduce_fusion
  264.9 1.9 copy.23
  (7 shorter events, 0.1 us)
Async XLA Ops:
  5.4 1.4 copy-start

commit v2 on v1

--- a/solution.py
+++ b/solution.py
@@ -8,6 +8,8 @@
 from jax.sharding import PartitionSpec as P
 
 VMEM_BYTES = 56 * 2**20
+STARTED = (0, 0, 3, 5, 7, 9, 11, 12, 13, 14)
+WINDOW = 15
 
 
 def term_parcel(flat_blocks, pack_rows, pack_keep, rows_out, per_shift):
@@ -166,12 +168,12 @@
     lax.fori_loop(0, steps, greet, 0)
     pl.semaphore_wait(barrier, steps)
 
-    def v_copy(chunk, target, send_sem):
+    def v_copy(chunk, target, send_sem, half):
         return pltpu.make_async_remote_copy(
-            src_ref=vall.at[chunk],
-            dst_ref=vall.at[chunk],
-            send_sem=send_sem,
-            recv_sem=v_recv.at[chunk],
+            src_ref=vall.at[chunk, half],
+            dst_ref=vall.at[chunk, half],
+            send_sem=send_sem.at[half],
+            recv_sem=v_recv.at[chunk, half],
             device_id={"wf": target},
         )
 
@@ -179,26 +181,26 @@
     core_peer = z * 4 + y * 2 + (1 - core)
     up, down = (me + 4) % nodes, (me + nodes - 4) % nodes
 
-    def wait_chunk(chunk):
-        v_copy(chunk, core_peer, y_send.at[0]).wait_recv()
-
-    def each_way(dz, action):
+    def wait_chunk(chunk, half):
+        v_copy(chunk, core_peer, y_send.at[0], half).wait_recv()
+
+    def each_way(dz, half, action):
         index = dz + z_count - 1
         chunk = me + 4 * dz
         if dz <= 0:
 
             @pl.when(z < z_count - 1)
             def _():
-                action(v_copy(chunk, up, v_send.at[index, 0]))
+                action(v_copy(chunk, up, v_send.at[index, 0], half))
 
         if dz >= 0:
 
             @pl.when(z > 0)
             def _():
-                action(v_copy(chunk, down, v_send.at[index, 1]))
-
-        action(v_copy(chunk, y_peer, v_send.at[index, 2]))
-        action(v_copy(chunk, core_peer, v_send.at[index, 3]))
+                action(v_copy(chunk, down, v_send.at[index, 1], half))
+
+        action(v_copy(chunk, y_peer, v_send.at[index, 2], half))
+        action(v_copy(chunk, core_peer, v_send.at[index, 3], half))
 
     def y_chunk(z_step):
         return ((z + z_step) % z_count) * 4 + (1 - y) * 2 + core
@@ -230,36 +232,54 @@
         r_copy(step).start()
         return carry
 
-    vall[me] = v_ref[...]
-    each_way(0, lambda copy: copy.start())
-    lax.fori_loop(0, nodes // 2, pack_and_send, 0)
+    def send(turn, carry):
+        step = steps - 1 - turn
+
+        @pl.when(turn >= WINDOW)
+        def _():
+            r_copy(step + WINDOW).wait_send()
+
+        pack(step, parcel)
+        r_copy(step).start()
+        return carry
 
     def inside(dz):
         return (z + dz >= 0) & (z + dz < z_count)
 
+    def relay(far, half):
+        for dz in (-far, far):
+
+            @pl.when(inside(dz))
+            def _(dz=dz):
+                wait_chunk(me + 4 * dz, half)
+                each_way(dz, half, lambda copy: copy.start())
+
+    def pass_on(z_step):
+        chunk = y_chunk(z_step)
+        for half in range(2):
+            wait_chunk(chunk, half)
+            v_copy(chunk, core_peer, y_send.at[z_step], half).start()
+
     others = [sign * far for far in range(1, z_count) for sign in (-1, 1)]
-    for dz in others:
-
-        @pl.when(inside(dz))
-        def _(dz=dz):
-            wait_chunk(me + 4 * dz)
-            each_way(dz, lambda copy: copy.start())
-
-    lax.fori_loop(nodes // 2, steps, pack_and_send, 0)
+    events = [functools.partial(relay, far, half) for far in range(1, z_count) for half in range(2)]
+    events += [functools.partial(pass_on, z_step) for z_step in range(z_count)]
+    vall[me] = v_ref[...]
+    for half in range(2):
+        each_way(0, half, lambda copy: copy.start())
+    begun = 0
+    for number, event in enumerate(events):
+        goal = min(steps, STARTED[number]) if number < len(STARTED) else steps
+        lax.fori_loop(begun, goal, send, 0)
+        begun = goal
+        event()
+    lax.fori_loop(begun, steps, send, 0)
     pack(steps, arrived)
-
-    def pass_on(z_step, carry):
-        chunk = y_chunk(z_step)
-        wait_chunk(chunk)
-        v_copy(chunk, core_peer, y_send.at[z_step]).start()
-        return carry
-
-    lax.fori_loop(0, z_count, pass_on, 0)
 
     def last_chunks(z_step, carry):
         z_from = (z + z_step) % z_count
-        wait_chunk(z_from * 4 + y * 2 + (1 - core))
-        wait_chunk(z_from * 4 + (1 - y) * 2 + (1 - core))
+        for half in range(2):
+            wait_chunk(z_from * 4 + y * 2 + (1 - core), half)
+            wait_chunk(z_from * 4 + (1 - y) * 2 + (1 - core), half)
         return carry
 
     lax.fori_loop(0, z_count, last_chunks, 0)
@@ -354,22 +374,29 @@
 
     lax.fori_loop(0, slots, finish, 0)
 
-    each_way(0, lambda copy: copy.wait_send())
+    for half in range(2):
+        each_way(0, half, lambda copy: copy.wait_send())
     for dz in others:
 
         @pl.when(inside(dz))
         def _(dz=dz):
-            each_way(dz, lambda copy: copy.wait_send())
+            for half in range(2):
+                each_way(dz, half, lambda copy: copy.wait_send())
 
     def sent_y(z_step, carry):
-        v_copy(y_chunk(z_step), core_peer, y_send.at[z_step]).wait_send()
+        for half in range(2):
+            v_copy(y_chunk(z_step), core_peer, y_send.at[z_step], half).wait_send()
         return carry
 
     lax.fori_loop(0, z_count, sent_y, 0)
 
     def sent(step, carry):
-        r_copy(step).wait_send()
         s_copy(me, step).wait_send()
+
+        @pl.when(step < min(WINDOW, steps))
+        def _():
+            r_copy(step).wait_send()
+
         return carry
 
     lax.fori_loop(0, steps, sent, 0)
@@ -417,9 +444,9 @@
             pltpu.VMEM((slots, side, count * side), jnp.float32),
             pltpu.VMEM((nodes, 8, count * side), jnp.float32),
             pltpu.SemaphoreType.DMA,
-            pltpu.SemaphoreType.DMA((nodes,)),
-            pltpu.SemaphoreType.DMA((2 * (nodes // 4) - 1, 4)),
-            pltpu.SemaphoreType.DMA((nodes // 4,)),
+            pltpu.SemaphoreType.DMA((nodes, 2)),
+            pltpu.SemaphoreType.DMA((2 * (nodes // 4) - 1, 4, 2)),
+            pltpu.SemaphoreType.DMA((nodes // 4, 2)),
             pltpu.SemaphoreType.DMA((nodes,)),
             pltpu.SemaphoreType.DMA((nodes,)),
             pltpu.SemaphoreType.DMA((nodes,)),

time: 267 us -> 191 us (0.72)
  Pallas kernels: 257 us -> 180 us
    pallas_call x1, Pallas kernels: 257 us -> 180 us  [node_program(): pl.pallas_call(functools.partial(node_kernel, (nodes, terms, shifts, slot...]
where the time goes in v2:
time: 191 us; the launch traced here: 190 us
  Pallas kernels  180 us (94%)
  local copies, waits for them, and re-layouts  5.84 us (3%)
  other arithmetic  3.43 us (2%)
    pallas_call x1, Pallas kernels, node_program(): pl.pallas_call(functools.partial(node_kernel, (nodes, terms, shifts, slot...  180 us

profile of v2, /device:TPU:0, one launch (start us, length us, event | category | flops | bytes accessed | tf_op | source)
XLA Modules:
  0.0 190.3 jit_solution(11717753087540475128)
XLA Ops:
  0.6 1.3 subtract_bitcast_fusion.energy
  1.9 0.7 add_select_fusion
  2.6 0.8 copy.21
  3.4 0.7 reshape.91.active
  4.1 0.1 reshape.90
  4.2 0.1 copy.17
  4.3 0.1 eq.58
  4.4 0.1 copy.18
  4.5 0.5 reduce_window_sum.11
  5.0 0.2 select_reduce_fusion
  5.2 0.1 copy.20
  5.3 0.1 squeeze.14.recv_cell
  5.4 0.0 copy-start
  5.4 0.7 select_reduce_fusion.1.place
  6.1 0.1 copy.19
  6.2 0.6 squeeze.13.send_item
  6.8 0.0 copy-done
  6.8 180.3 %shard_map.77 = (bf16[2,8,128,128]{3,2,1,0:T(8,128)(2,1)}, f32[2,128]{1,0:T(2,128)}) custom-call(s32[64]{0:T(128)} %squeeze.13.send_item, s32[64]{0:T(128)} %copy-done, s32[64]{0:T(128)} %select_reduce_fusion.1.place, s32[168]{0:T(256)} %reshape.91.active, f32[8]{0:T(128)} %subtract_bitcast_fusion.energy, bf16[2,8,128,128]{3,2,1,0:T(8,128)(2,1)} %v_ref.1, ...), custom_call_target="tpu_custom_call" | custom-call | flops 3221225472 | bytes 11010048 | tf_op jit(solution)/shard_map/pallas_call | solution.py:430
  187.1 1.3 slice_reduce_fusion
  188.4 1.9 copy.23
  (7 shorter events, 0.1 us)
Async XLA Ops:
  5.4 1.4 copy-start
